TPU v7x, 512 devices: a whole 4x8x8 slice. The times are simulated.
512 devices in a mesh: blk: 32 (over y, x_lo, core), uly: 16 (over x_hi, z).
Axes of the slice: x: 4 (x_hi: 2, x_lo: 2; x = x_hi * 2 + x_lo), y: 8, z: 8, core: 2. Of those that a mesh axis runs over, the one named last changes fastest.
Arguments:
- query_states: bfloat16 [65536, 2048], P(('blk', 'uly')), may hold values from -16 to 16
- key_matrix: bfloat16 [65536, 512], P(('blk', 'uly')), may hold values from -16 to 16
- value_matrix: bfloat16 [65536, 512], P(('blk', 'uly')), may hold values from -6 to 6
- layer_output: bfloat16 [65536, 2048], P(('blk', 'uly')), may hold values from -4 to 4
- output_grad: bfloat16 [65536, 2048], P(('blk', 'uly')), may hold values from -6 to 6
- stretch_order: int32 [64], replicated, may hold values from 0 to 63, each once
- document_ids: int32 [65536], replicated, may hold values from 0 to 1023, never falling along the last dimension, each value on 1 to 128 neighbouring positions
Outputs:
- query_grad: bfloat16 [65536, 2048], P(('blk', 'uly'))
- key_grad: bfloat16 [65536, 512], P(('blk', 'uly'))
- value_grad: bfloat16 [65536, 512], P(('blk', 'uly'))
Inputs may be any that keep to these rules, and one draw needn't show every extreme that they name: A permutation: each of 0 to 63 appears once; stored block c of 1024 rows holds the true positions stretch_order[c] * 1024 onward, in order. `document_ids`: never falling along the true positions; every document has 1 to 128 positions and one has exactly 128.
All inputs are finite; a program needn't handle non-finite values.
Results may differ from a plain program's by a relative error of at most 0.012.
Values may be sent and summed in bfloat16 or wider, within the bound.
A program may use at most 128 MiB of HBM per device.

v0:
```python
import math

import jax
import jax.numpy as jnp
from jax import lax
from jax.sharding import PartitionSpec as P

QUERY_HEADS = 16
KEY_VALUE_HEADS = 4
HEAD_SIZE = 128
DOC_MOST = 128


NEGATIVE = -1e30


def visibility(query_position, query_document, key_position, key_document):
    both = (key_position[None, :] <= query_position[:, None]) & (
        key_document[None, :] == query_document[:, None]
    )
    return both[:, None, :]


def logits(query_block, key_block, softmax_scale):
    return softmax_scale * jnp.einsum(
        "qhd,khd->qhk", query_block, key_block, preferred_element_type=jnp.float32
    )


def tile_grads(query_side, key_side, softmax_scale):
    query_block, grad_block, mass_block, sum_block, query_position, query_document = query_side
    key_block, value_block, key_position, key_document = key_side
    visible = visibility(query_position, query_document, key_position, key_document)
    probability = jnp.where(
        visible,
        jnp.exp(logits(query_block, key_block, softmax_scale) - mass_block[:, :, None]),
        0.0,
    )
    weight_grad = jnp.einsum(
        "qhd,khd->qhk", grad_block, value_block, preferred_element_type=jnp.float32
    )
    slopes = (probability * (weight_grad - sum_block[:, :, None])).astype(jnp.bfloat16)
    query_part = jnp.einsum("qhk,khd->qhd", slopes, key_block, preferred_element_type=jnp.float32)
    key_part = jnp.einsum("qhk,qhd->khd", slopes, query_block, preferred_element_type=jnp.float32)
    value_part = jnp.einsum(
        "qhk,qhd->khd",
        probability.astype(jnp.bfloat16),
        grad_block,
        preferred_element_type=jnp.float32,
    )
    return (query_part, key_part, value_part)


def per_device(
    query_states, key_matrix, value_matrix, layer_output, output_grad, stretch_order, document_ids
):
    token_count = query_states.shape[0]
    group_width = QUERY_HEADS // KEY_VALUE_HEADS
    softmax_scale = 1.0 / math.sqrt(HEAD_SIZE)
    reach_rows = DOC_MOST

    def separate_heads(tensor, head_count):
        return tensor.reshape(token_count, head_count, HEAD_SIZE)

    query_rows, key_rows, value_rows, grad_rows, output_rows = (
        lax.all_to_all(
            separate_heads(query_states, QUERY_HEADS),
            "uly",
            split_axis=1,
            concat_axis=0,
            tiled=True,
        ),
        lax.all_to_all(
            jnp.repeat(separate_heads(key_matrix, KEY_VALUE_HEADS), group_width, axis=1),
            "uly",
            split_axis=1,
            concat_axis=0,
            tiled=True,
        ),
        lax.all_to_all(
            jnp.repeat(separate_heads(value_matrix, KEY_VALUE_HEADS), group_width, axis=1),
            "uly",
            split_axis=1,
            concat_axis=0,
            tiled=True,
        ),
        lax.all_to_all(
            separate_heads(output_grad, QUERY_HEADS), "uly", split_axis=1, concat_axis=0, tiled=True
        ),
        lax.all_to_all(
            separate_heads(layer_output, QUERY_HEADS),
            "uly",
            split_axis=1,
            concat_axis=0,
            tiled=True,
        ),
    )
    row_count = query_rows.shape[0]
    stretch_rows = row_count // 2
    block_rows = min(stretch_rows, 512)
    block_count = stretch_rows // block_rows
    heads_here = query_rows.shape[1]
    stretches = stretch_order.shape[0]
    device = lax.axis_index("blk")
    stored_numbers = jnp.arange(stretches, dtype=jnp.int32)

    def query_start(member, number):
        return member * stretch_rows + number * block_rows

    def key_span(member, number):
        first = member * stretch_rows + max(0, number * block_rows - reach_rows)
        return slice(first, member * stretch_rows + (number + 1) * block_rows)

    def stored_of(true_stretch):
        return jnp.sum(jnp.where(stretch_order == true_stretch, stored_numbers, 0))

    def continues(true_stretch):
        first_row = jnp.clip(true_stretch, 1, stretches - 1) * stretch_rows
        before = lax.dynamic_index_in_dim(document_ids, first_row - 1, 0, keepdims=False)
        after = lax.dynamic_index_in_dim(document_ids, first_row, 0, keepdims=False)
        return (true_stretch >= 1) & (true_stretch < stretches) & (before == after)

    def place(true_stretch, offset, length):
        first_row = true_stretch * stretch_rows + offset
        return (
            first_row + jnp.arange(length, dtype=jnp.int32),
            lax.dynamic_slice_in_dim(document_ids, first_row, length, 0),
        )

    def pick(tensor, number):
        return lax.dynamic_slice_in_dim(tensor, number * reach_rows, reach_rows, 0)

    home_true = [
        lax.dynamic_index_in_dim(stretch_order, 2 * device + member, 0, keepdims=False)
        for member in range(2)
    ]
    placed = [place(home_true[member], 0, stretch_rows) for member in range(2)]
    home_position = jnp.concatenate([placed[0][0], placed[1][0]])
    home_document = jnp.concatenate([placed[0][1], placed[1][1]])

    def update(softmax_stats, row_first, row_total, key_block, key_position, key_document):
        row_peak, row_mass = softmax_stats
        picked = slice(row_first, row_first + row_total)
        visible = visibility(
            home_position[picked], home_document[picked], key_position, key_document
        )
        masked = jnp.where(visible, logits(query_rows[picked], key_block, softmax_scale), NEGATIVE)
        old_peak = row_peak[picked]
        old_mass = row_mass[picked]
        new_peak = jnp.maximum(old_peak, jnp.max(masked, axis=2))
        new_mass = old_mass * jnp.exp(old_peak - new_peak) + jnp.sum(
            jnp.where(visible, jnp.exp(masked - new_peak[:, :, None]), 0.0), axis=2
        )
        return (row_peak.at[picked].set(new_peak), row_mass.at[picked].set(new_mass))

    softmax_stats = (
        jnp.full((row_count, heads_here), NEGATIVE, jnp.float32),
        jnp.zeros((row_count, heads_here), jnp.float32),
    )
    for member in range(2):
        for number in range(block_count):
            keys_here = key_span(member, number)
            softmax_stats = update(
                softmax_stats,
                query_start(member, number),
                block_rows,
                key_rows[keys_here],
                home_position[keys_here],
                home_document[keys_here],
            )
    tail_keys = jnp.concatenate(
        [
            key_rows[(member + 1) * stretch_rows - reach_rows : (member + 1) * stretch_rows]
            for member in range(2)
        ],
        axis=0,
    )
    tail_values = jnp.concatenate(
        [
            value_rows[(member + 1) * stretch_rows - reach_rows : (member + 1) * stretch_rows]
            for member in range(2)
        ],
        axis=0,
    )
    head_queries = jnp.concatenate(
        [
            query_rows[member * stretch_rows : member * stretch_rows + reach_rows]
            for member in range(2)
        ],
        axis=0,
    )
    head_grads = jnp.concatenate(
        [
            grad_rows[member * stretch_rows : member * stretch_rows + reach_rows]
            for member in range(2)
        ],
        axis=0,
    )
    all_tail_keys, all_tail_values = (
        lax.all_gather(tail_keys, "blk", axis=0, tiled=True),
        lax.all_gather(tail_values, "blk", axis=0, tiled=True),
    )
    before_needed = []
    before_keys = []
    for member in range(2):
        before_true = home_true[member] - 1
        before_stored = stored_of(before_true)
        needed = continues(home_true[member])
        key_block = pick(all_tail_keys, before_stored)
        value_block = pick(all_tail_values, before_stored)
        key_position, key_document = place(before_true, stretch_rows - reach_rows, reach_rows)
        before_needed.append(needed)
        before_keys.append((key_block, value_block, key_position, key_document))
        softmax_stats = lax.cond(
            needed,
            lambda running, member=member, key_block=key_block, key_position=key_position, key_document=key_document: update(
                running, member * stretch_rows, reach_rows, key_block, key_position, key_document
            ),
            lambda unchanged: unchanged,
            softmax_stats,
        )
    row_peak, row_mass = softmax_stats
    log_mass = row_peak + jnp.log(row_mass)
    grad_sum = jnp.einsum("qhd,qhd->qh", grad_rows, output_rows, preferred_element_type=jnp.float32)
    head_mass = jnp.concatenate(
        [
            log_mass[member * stretch_rows : member * stretch_rows + reach_rows]
            for member in range(2)
        ],
        axis=0,
    )
    head_sums = jnp.concatenate(
        [
            grad_sum[member * stretch_rows : member * stretch_rows + reach_rows]
            for member in range(2)
        ],
        axis=0,
    )
    all_head_queries, all_head_grads = (
        lax.all_gather(head_queries, "blk", axis=0, tiled=True),
        lax.all_gather(head_grads, "blk", axis=0, tiled=True),
    )
    all_head_mass, all_head_sums = (
        lax.all_gather(head_mass, "blk", axis=0, tiled=True),
        lax.all_gather(head_sums, "blk", axis=0, tiled=True),
    )
    zero_rows = jnp.zeros((row_count, heads_here, HEAD_SIZE), jnp.float32)
    query_acc, key_acc, value_acc = (zero_rows, zero_rows, zero_rows)
    for member in range(2):
        for number in range(block_count):
            query_first = query_start(member, number)
            rows_here = slice(query_first, query_first + block_rows)
            keys_here = key_span(member, number)
            query_part, key_part, value_part = tile_grads(
                (
                    query_rows[rows_here],
                    grad_rows[rows_here],
                    log_mass[rows_here],
                    grad_sum[rows_here],
                    home_position[rows_here],
                    home_document[rows_here],
                ),
                (
                    key_rows[keys_here],
                    value_rows[keys_here],
                    home_position[keys_here],
                    home_document[keys_here],
                ),
                softmax_scale,
            )
            query_acc = query_acc.at[rows_here].add(query_part)
            key_acc = key_acc.at[keys_here].add(key_part)
            value_acc = value_acc.at[keys_here].add(value_part)
    for member in range(2):
        head_picked = slice(member * stretch_rows, member * stretch_rows + reach_rows)
        query_side = (
            query_rows[head_picked],
            grad_rows[head_picked],
            log_mass[head_picked],
            grad_sum[head_picked],
            home_position[head_picked],
            home_document[head_picked],
        )

        def before_part(
            running, query_side=query_side, key_side=before_keys[member], head_picked=head_picked
        ):
            query_part = tile_grads(query_side, key_side, softmax_scale)[0]
            return running.at[head_picked].add(query_part)

        query_acc = lax.cond(
            before_needed[member], before_part, lambda unchanged: unchanged, query_acc
        )
        after_true = home_true[member] + 1
        after_stored = stored_of(after_true)
        after_needed = continues(after_true)
        after_position, after_document = place(after_true, 0, reach_rows)
        after_side = (
            pick(all_head_queries, after_stored),
            pick(all_head_grads, after_stored),
            pick(all_head_mass, after_stored),
            pick(all_head_sums, after_stored),
            after_position,
            after_document,
        )
        tail_picked = slice((member + 1) * stretch_rows - reach_rows, (member + 1) * stretch_rows)
        key_side = (
            key_rows[tail_picked],
            value_rows[tail_picked],
            home_position[tail_picked],
            home_document[tail_picked],
        )

        def after_part(running, after_side=after_side, key_side=key_side, tail_picked=tail_picked):
            unused, key_part, value_part = tile_grads(after_side, key_side, softmax_scale)
            return (
                running[0].at[tail_picked].add(key_part),
                running[1].at[tail_picked].add(value_part),
            )

        key_acc, value_acc = lax.cond(
            after_needed, after_part, lambda unchanged: unchanged, (key_acc, value_acc)
        )
    query_grad_rows = (softmax_scale * query_acc).astype(jnp.bfloat16)
    query_grad = lax.all_to_all(
        query_grad_rows, "uly", split_axis=0, concat_axis=1, tiled=True
    ).reshape(token_count, QUERY_HEADS * HEAD_SIZE)
    key_positions_list, value_positions_list = (
        lax.all_to_all(
            (softmax_scale * key_acc).astype(jnp.bfloat16),
            "uly",
            split_axis=0,
            concat_axis=1,
            tiled=True,
        ).astype(jnp.float32),
        lax.all_to_all(
            value_acc.astype(jnp.bfloat16), "uly", split_axis=0, concat_axis=1, tiled=True
        ).astype(value_acc.dtype),
    )
    key_grad = (
        key_positions_list.reshape(token_count, KEY_VALUE_HEADS, group_width, HEAD_SIZE)
        .sum(axis=2)
        .reshape(token_count, KEY_VALUE_HEADS * HEAD_SIZE)
        .astype(jnp.bfloat16)
    )
    value_grad = (
        value_positions_list.reshape(token_count, KEY_VALUE_HEADS, group_width, HEAD_SIZE)
        .sum(axis=2)
        .reshape(token_count, KEY_VALUE_HEADS * HEAD_SIZE)
        .astype(jnp.bfloat16)
    )
    return (query_grad, key_grad, value_grad)


def solution(mesh):
    placed = (
        P(("blk", "uly"), None),
        P(("blk", "uly"), None),
        P(("blk", "uly"), None),
        P(("blk", "uly"), None),
        P(("blk", "uly"), None),
        P(),
        P(),
    )
    return jax.shard_map(
        per_device,
        mesh=mesh,
        in_specs=placed,
        out_specs=(P(("blk", "uly"), None), P(("blk", "uly"), None), P(("blk", "uly"), None)),
        check_vma=False,
    )
```

profile of v0, /device:TPU:8, one launch (start us, length us, event | category | flops | bytes accessed | tf_op | source)
XLA Modules:
  0.0 396.0 jit_solution(13967950395348444652)
XLA Ops:
  8.2 29.9 %all_to_all.111 = bf16[128,16,128]{2,0,1:T(8,128)(2,1)S(1)} all-to-all(bf16[128,16,128]{2,0,1:T(8,128)(2,1)S(1)} %bitcast.805), channel_id=1, replica_groups=mesh['blk'=32,'uly'=16] {'uly'}, dimensions={1} | all-to-all | bytes 1048576 | tf_op jit(solution)/shard_map/all_to_all | solution.py:73
  39.7 4.5 %all-to-all-start.2 = ((bf16[128,16,128]{2,0,1:T(8,128)(2,1)}), bf16[128,16,128]{2,0,1:T(8,128)(2,1)S(1)}, u32[]{:S(2)}, u32[]{:S(2)}) async-start(bf16[128,16,128]{2,0,1:T(8,128)(2,1)} %bitcast.125), calls=%async_computation.2 | async-start | bytes 1048576 | tf_op jit(solution)/shard_map/all_to_all | solution.py:80
  45.3 15.0 %all-to-all-done.2 = bf16[128,16,128]{2,0,1:T(8,128)(2,1)S(1)} async-done(((bf16[128,16,128]{2,0,1:T(8,128)(2,1)}), bf16[128,16,128]{2,0,1:T(8,128)(2,1)S(1)}, u32[]{:S(2)}, u32[]{:S(2)}) %all-to-all-start.2) | async-done | bytes 524320 | tf_op jit(solution)/shard_map/all_to_all | solution.py:80
  60.4 5.1 %all-to-all-start.3 = ((bf16[128,16,128]{0,2,1:T(8,128)(2,1)}), bf16[128,16,128]{0,2,1:T(8,128)(2,1)S(1)}, u32[]{:S(2)}, u32[]{:S(2)}) async-start(bf16[128,16,128]{0,2,1:T(8,128)(2,1)} %bitcast.129), calls=%async_computation.3 | async-start | bytes 1048576 | tf_op jit(solution)/shard_map/all_to_all | solution.py:87
  67.9 13.0 %all-to-all-done.3 = bf16[128,16,128]{0,2,1:T(8,128)(2,1)S(1)} async-done(((bf16[128,16,128]{0,2,1:T(8,128)(2,1)}), bf16[128,16,128]{0,2,1:T(8,128)(2,1)S(1)}, u32[]{:S(2)}, u32[]{:S(2)}) %all-to-all-start.3) | async-done | bytes 524320 | tf_op jit(solution)/shard_map/all_to_all | solution.py:87
  80.9 5.1 %all-to-all-start.1 = ((bf16[128,16,128]{0,2,1:T(8,128)(2,1)}), bf16[128,16,128]{0,2,1:T(8,128)(2,1)S(1)}, u32[]{:S(2)}, u32[]{:S(2)}) async-start(bf16[128,16,128]{0,2,1:T(8,128)(2,1)} %bitcast.87), calls=%async_computation.1 | async-start | bytes 1048576 | tf_op jit(solution)/shard_map/all_to_all | solution.py:66
  94.8 6.7 %all-to-all-done.1 = bf16[128,16,128]{0,2,1:T(8,128)(2,1)S(1)} async-done(((bf16[128,16,128]{0,2,1:T(8,128)(2,1)}), bf16[128,16,128]{0,2,1:T(8,128)(2,1)S(1)}, u32[]{:S(2)}, u32[]{:S(2)}) %all-to-all-start.1) | async-done | bytes 524320 | tf_op jit(solution)/shard_map/all_to_all | solution.py:66
  101.4 5.1 %all-to-all-start.4 = ((bf16[128,16,128]{0,2,1:T(8,128)(2,1)}), bf16[128,16,128]{0,2,1:T(8,128)(2,1)S(1)}, u32[]{:S(2)}, u32[]{:S(2)}) async-start(bf16[128,16,128]{0,2,1:T(8,128)(2,1)} %bitcast.136), calls=%async_computation.4 | async-start | bytes 1048576 | tf_op jit(solution)/shard_map/all_to_all | solution.py:90
  114.5 1.5 fusion.218
  134.0 1.4 fusion.187
  139.4 1.7 copy.211
  141.1 1.7 copy.212
  142.8 1.7 copy.213
  146.4 2.1 select_reduce_fusion.4
  150.1 34.3 %all_gather.23 = f32[8192,1]{0,1:T(1,128)} all-gather(f32[256,1]{0,1:T(1,128)S(1)} %pad_maximum_fusion.5), channel_id=1, replica_groups=mesh['blk'=32,'uly'=16] {'blk'}, dimensions={0}, use_global_device_ids=true | all-gather | bytes 33792 | tf_op jit(solution)/shard_map/all_gather | solution.py:245
  188.6 2.5 conditional.6
  191.1 2.7 conditional.7
  201.1 3.4 conditional.8
  204.5 3.4 conditional.9
  210.6 10.3 %all-to-all-start.5 = ((bf16[16,2,8192]{2,1,0:T(2,128)(2,1)}), bf16[16,2,8192]{2,1,0:T(2,128)(2,1)}, u32[]{:S(2)}, u32[]{:S(2)}) async-start(bf16[16,2,8192]{2,1,0:T(2,128)(2,1)} %reshape.2305), calls=%async_computation.5 | async-start | bytes 1048576 | tf_op jit(solution)/shard_map/all_to_all | solution.py:325
  227.8 30.5 %all_gather.21 = f32[8192,1]{0,1:T(1,128)S(1)} all-gather(f32[256,1]{0,1:T(1,128)S(1)} %pad_maximum_fusion.4), channel_id=1, replica_groups=mesh['blk'=32,'uly'=16] {'blk'}, dimensions={0}, use_global_device_ids=true | all-gather | bytes 33792 | tf_op jit(solution)/shard_map/all_gather | solution.py:244
  258.2 53.8 %all-gather.11.cloned.1.call-done = bf16[8192,1,128]{0,2,1:T(8,128)(2,1)} async-done(((bf16[256,1,128]{0,2,1:T(8,128)(2,1)}), bf16[8192,1,128]{0,2,1:T(8,128)(2,1)}) %all-gather.11.cloned.1.call-update) | async-done | bytes 2097168 | tf_op jit(solution)/shard_map/all_gather | solution.py:241
  312.0 7.9 %conditional.10 = (f32[2048,1,128]{2,0,1:T(8,128)S(1)}, f32[2048,1,128]{2,0,1:T(8,128)S(1)}, (f32[2048,1,128]{0,2,1:T(8,128)S(1)}, f32[2048,1,128]{0,2,1:T(8,128)})) conditional(s32[]{:T(128)} %convert_element_type.134, (f32[2048,1,128]{2,0,1:T(8,128)S(1)}, f32[2048,1,128]{2,0,1:T(8,128)S(1)}) %tuple.191, ...), branch_computations={%region_23.24_spmd.clone, %region_24.25_spmd.clone.clone} | conditional | flops 16973956 | bytes 4861014 | solution.py:321
  320.0 16.5 %conditional.11 = (f32[2048,1,128]{0,2,1:T(8,128)}, f32[2048,1,128]{2,0,1:T(8,128)S(1)}) conditional(s32[]{:T(128)} %convert_element_type.133, (f32[2048,1,128]{0,2,1:T(8,128)S(1)}, f32[2048,1,128]{0,2,1:T(8,128)}) %get-tuple-element.1140, (f32[2048,1,128]{2,0,1:T(8,128)S(1)}, s32[]{:T(128)}, s32[64]{0:T(128)S(1)}, s32[64]{0:T(128)S(1)}, ...), branch_computations={%region_25.26_spmd, %region_26.28_spmd} | conditional | flops 16974152 | bytes 23735204 | solution.py:321
  325.3 4.2 %copy.227 = bf16[8192,1,128]{2,0,1:T(8,128)(2,1)} copy(bf16[8192,1,128]{0,2,1:T(8,128)(2,1)} %get-tuple-element.1121) | data formatting | bytes 4194304 | tf_op jit(solution)/shard_map
  330.5 2.5 copy.228
  333.0 1.7 fusion.43
  338.5 10.0 %all-to-all-start.6 = ((bf16[16,2,8192]{2,1,0:T(2,128)(2,1)}), bf16[16,2,8192]{2,1,0:T(2,128)(2,1)S(1)}, u32[]{:S(2)}, u32[]{:S(2)}) async-start(bf16[16,2,8192]{2,1,0:T(2,128)(2,1)} %reshape.2307), calls=%async_computation.6 | async-start | bytes 1048576 | tf_op jit(solution)/shard_map/all_to_all | solution.py:329
  352.0 13.9 %all-to-all-done.6 = bf16[16,2,8192]{2,1,0:T(2,128)(2,1)S(1)} async-done(((bf16[16,2,8192]{2,1,0:T(2,128)(2,1)}), bf16[16,2,8192]{2,1,0:T(2,128)(2,1)S(1)}, u32[]{:S(2)}, u32[]{:S(2)}) %all-to-all-start.6) | async-done | bytes 524320 | tf_op jit(solution)/shard_map/all_to_all | solution.py:329
  365.9 4.8 %all-to-all-start.7 = ((bf16[16,2,8192]{2,1,0:T(2,128)(2,1)}), bf16[16,2,8192]{2,1,0:T(2,128)(2,1)S(1)}, u32[]{:S(2)}, u32[]{:S(2)}) async-start(bf16[16,2,8192]{2,1,0:T(2,128)(2,1)} %reshape.2309), calls=%async_computation.7 | async-start | bytes 1048576 | tf_op jit(solution)/shard_map/all_to_all | solution.py:336
  370.8 2.2 reshape.2306
  376.0 11.9 %all-to-all-done.7 = bf16[16,2,8192]{2,1,0:T(2,128)(2,1)S(1)} async-done(((bf16[16,2,8192]{2,1,0:T(2,128)(2,1)}), bf16[16,2,8192]{2,1,0:T(2,128)(2,1)S(1)}, u32[]{:S(2)}, u32[]{:S(2)}) %all-to-all-start.7) | async-done | bytes 524320 | tf_op jit(solution)/shard_map/all_to_all | solution.py:336
  (434 shorter events, 89.7 us)
Async XLA Ops:
  7.2 31.6 %copy-start.43 = (bf16[128,512]{1,0:T(8,128)(2,1)S(1)}, bf16[128,512]{1,0:T(8,128)(2,1)}, u32[]{:S(2)}) copy-start(bf16[128,512]{1,0:T(8,128)(2,1)} %param.81) | copy-start | bytes 393220
  7.2 180.0 %all-gather.5.cloned.1.call-start = ((), (), s32[]{:S(2)}) async-start(), calls=%async_computation.8 | async-start | bytes 2162688 | tf_op jit(solution)/shard_map/all_gather | solution.py:200
  39.7 20.6 %all-to-all-start.2 = ((bf16[128,16,128]{2,0,1:T(8,128)(2,1)}), bf16[128,16,128]{2,0,1:T(8,128)(2,1)S(1)}, u32[]{:S(2)}, u32[]{:S(2)}) async-start(bf16[128,16,128]{2,0,1:T(8,128)(2,1)} %bitcast.125), calls=%async_computation.2 | async-start | bytes 1048576 | tf_op jit(solution)/shard_map/all_to_all | solution.py:80
  60.4 20.5 %all-to-all-start.3 = ((bf16[128,16,128]{0,2,1:T(8,128)(2,1)}), bf16[128,16,128]{0,2,1:T(8,128)(2,1)S(1)}, u32[]{:S(2)}, u32[]{:S(2)}) async-start(bf16[128,16,128]{0,2,1:T(8,128)(2,1)} %bitcast.129), calls=%async_computation.3 | async-start | bytes 1048576 | tf_op jit(solution)/shard_map/all_to_all | solution.py:87
  65.5 24.4 %copy-start.25 = (bf16[128,2048]{1,0:T(8,128)(2,1)S(1)}, bf16[128,2048]{1,0:T(8,128)(2,1)}, u32[]{:S(2)}) copy-start(bf16[128,2048]{1,0:T(8,128)(2,1)} %param.82) | copy-start | bytes 1572868
  65.5 135.3 %all-gather.7.cloned.1.call-start = ((), (), s32[]{:S(2)}) async-start(), calls=%async_computation.9 | async-start | bytes 2162688 | tf_op jit(solution)/shard_map/all_gather | solution.py:201
  80.9 20.6 %all-to-all-start.1 = ((bf16[128,16,128]{0,2,1:T(8,128)(2,1)}), bf16[128,16,128]{0,2,1:T(8,128)(2,1)S(1)}, u32[]{:S(2)}, u32[]{:S(2)}) async-start(bf16[128,16,128]{0,2,1:T(8,128)(2,1)} %bitcast.87), calls=%async_computation.1 | async-start | bytes 1048576 | tf_op jit(solution)/shard_map/all_to_all | solution.py:66
  92.8 31.3 %copy-start.64 = (s32[1024]{0:T(1024)}, s32[1024]{0:T(1024)S(1)}, u32[]{:S(2)}) copy-start(s32[1024]{0:T(1024)S(1)} %iota_add_fusion.1) | copy-start | bytes 12292
  92.8 31.3 %copy-start.62 = (s32[1024]{0:T(1024)}, s32[1024]{0:T(1024)S(1)}, u32[]{:S(2)}) copy-start(s32[1024]{0:T(1024)S(1)} %iota_add_fusion) | copy-start | bytes 12292
  93.5 30.6 %copy-start.63 = (s32[1024]{0:T(1024)}, s32[1024]{0:T(1024)S(1)}, u32[]{:S(2)}) copy-start(s32[1024]{0:T(1024)S(1)} %get-tuple-element.1322) | copy-start | bytes 12292
  93.5 30.6 %copy-start.65 = (s32[1024]{0:T(1024)}, s32[1024]{0:T(1024)S(1)}, u32[]{:S(2)}) copy-start(s32[1024]{0:T(1024)S(1)} %get-tuple-element.1323) | copy-start | bytes 12292
  94.8 37.3 %copy-start.66 = (s32[512]{0:T(512)}, s32[512]{0:T(512)S(1)}, u32[]{:S(2)}) copy-start(s32[512]{0:T(512)S(1)} %get-tuple-element.1341) | copy-start | bytes 6148
  101.4 27.3 %all-to-all-start.4 = ((bf16[128,16,128]{0,2,1:T(8,128)(2,1)}), bf16[128,16,128]{0,2,1:T(8,128)(2,1)S(1)}, u32[]{:S(2)}, u32[]{:S(2)}) async-start(bf16[128,16,128]{0,2,1:T(8,128)(2,1)} %bitcast.136), calls=%async_computation.4 | async-start | bytes 1048576 | tf_op jit(solution)/shard_map/all_to_all | solution.py:90
  106.6 151.6 %all-gather.9.cloned.1.call-start = ((), (), s32[]{:S(2)}) async-start(), calls=%async_computation.10 | async-start | bytes 2162688 | tf_op jit(solution)/shard_map/all_gather | solution.py:240
  133.9 178.1 %all-gather.11.cloned.1.call-start = ((), (), s32[]{:S(2)}) async-start(), calls=%async_computation.11 | async-start | bytes 2162688 | tf_op jit(solution)/shard_map/all_gather | solution.py:241
  148.5 35.9 %copy-start.39 = (bf16[128,1,128]{0,2,1:T(8,128)(2,1)S(1)}, bf16[128,1,128]{0,2,1:T(8,128)(2,1)}, u32[]{:S(2)}) copy-start(bf16[128,1,128]{0,2,1:T(8,128)(2,1)} %get-tuple-element.1289) | copy-start | bytes 98308
  148.5 35.9 %copy-start.54 = (bf16[128,1,128]{0,2,1:T(8,128)(2,1)S(1)}, bf16[128,1,128]{0,2,1:T(8,128)(2,1)}, u32[]{:S(2)}) copy-start(bf16[128,1,128]{0,2,1:T(8,128)(2,1)} %copy.221) | copy-start | bytes 98308
  149.4 39.2 %copy-start.108 = (s32[128]{0:T(128)S(1)}, s32[128]{0:T(128)}, u32[]{:S(2)}) copy-start(s32[128]{0:T(128)} %get-tuple-element.1321) | copy-start | bytes 1540
  149.4 39.2 %copy-start.125 = (s32[128]{0:T(128)S(1)}, s32[128]{0:T(128)}, u32[]{:S(2)}) copy-start(s32[128]{0:T(128)} %iota_add_fusion.3) | copy-start | bytes 1540
  149.4 41.6 %copy-start.106 = (s32[128]{0:T(128)S(1)}, s32[128]{0:T(128)}, u32[]{:S(2)}) copy-start(s32[128]{0:T(128)} %get-tuple-element.1320) | copy-start | bytes 1540
  149.5 41.6 %copy-start.127 = (s32[128]{0:T(128)S(1)}, s32[128]{0:T(128)}, u32[]{:S(2)}) copy-start(s32[128]{0:T(128)} %iota_add_fusion.2) | copy-start | bytes 1540
  149.5 44.4 %copy-start.12 = (f32[512,1,512]{0,2,1:T(8,128)S(1)}, f32[512,1,512]{0,2,1:T(8,128)}, u32[]{:S(2)}) copy-start(f32[512,1,512]{0,2,1:T(8,128)} %copy-done.11) | copy-start | bytes 3145732
  150.0 41.1 %copy-start.102 = (f32[128,1]{0,1:T(1,128)}, f32[128,1]{0,1:T(1,128)S(1)}, u32[]{:S(2)}) copy-start(f32[128,1]{0,1:T(1,128)S(1)} %get-tuple-element.1324) | copy-start | bytes 1540
  150.0 41.1 %copy-start.104 = (f32[128,1]{0,1:T(1,128)}, f32[128,1]{0,1:T(1,128)S(1)}, u32[]{:S(2)}) copy-start(f32[128,1]{0,1:T(1,128)S(1)} %get-tuple-element.1325) | copy-start | bytes 1540
  150.0 43.9 %copy-start.44 = (bf16[4,128,1,128]{3,1,0,2:T(8,128)(2,1)S(1)}, bf16[4,128,1,128]{3,1,0,2:T(8,128)(2,1)}, u32[]{:S(2)}) copy-start(bf16[4,128,1,128]{3,1,0,2:T(8,128)(2,1)} %copy.207) | copy-start | bytes 393220
  150.0 43.9 %copy-start.67 = (s32[512]{0:T(512)S(1)}, s32[512]{0:T(512)}, u32[]{:S(2)}) copy-start(s32[512]{0:T(512)} %copy-done.66) | copy-start | bytes 6148
  150.0 43.9 %copy-start.78 = (s32[512]{0:T(512)S(1)}, s32[512]{0:T(512)}, u32[]{:S(2)}) copy-start(s32[512]{0:T(512)} %copy-done.77) | copy-start | bytes 6148
  210.6 127.9 %all-to-all-start.5 = ((bf16[16,2,8192]{2,1,0:T(2,128)(2,1)}), bf16[16,2,8192]{2,1,0:T(2,128)(2,1)}, u32[]{:S(2)}, u32[]{:S(2)}) async-start(bf16[16,2,8192]{2,1,0:T(2,128)(2,1)} %reshape.2305), calls=%async_computation.5 | async-start | bytes 1048576 | tf_op jit(solution)/shard_map/all_to_all | solution.py:325
  227.1 84.8 %copy-start.38 = (bf16[128,1,128]{2,0,1:T(8,128)(2,1)S(1)}, bf16[128,1,128]{2,0,1:T(8,128)(2,1)}, u32[]{:S(2)}) copy-start(bf16[128,1,128]{2,0,1:T(8,128)(2,1)} %copy-done.37) | copy-start | bytes 98308
  227.1 84.8 %copy-start.58 = (bf16[128,1,128]{2,0,1:T(8,128)(2,1)S(1)}, bf16[128,1,128]{2,0,1:T(8,128)(2,1)}, u32[]{:S(2)}) copy-start(bf16[128,1,128]{2,0,1:T(8,128)(2,1)} %copy-done.57) | copy-start | bytes 98308
  338.5 27.4 %all-to-all-start.6 = ((bf16[16,2,8192]{2,1,0:T(2,128)(2,1)}), bf16[16,2,8192]{2,1,0:T(2,128)(2,1)S(1)}, u32[]{:S(2)}, u32[]{:S(2)}) async-start(bf16[16,2,8192]{2,1,0:T(2,128)(2,1)} %reshape.2307), calls=%async_computation.6 | async-start | bytes 1048576 | tf_op jit(solution)/shard_map/all_to_all | solution.py:329
  365.9 21.9 %all-to-all-start.7 = ((bf16[16,2,8192]{2,1,0:T(2,128)(2,1)}), bf16[16,2,8192]{2,1,0:T(2,128)(2,1)S(1)}, u32[]{:S(2)}, u32[]{:S(2)}) async-start(bf16[16,2,8192]{2,1,0:T(2,128)(2,1)} %reshape.2309), calls=%async_computation.7 | async-start | bytes 1048576 | tf_op jit(solution)/shard_map/all_to_all | solution.py:336
  (108 other events, 328.8 us)
Sparse Core Ops, SparseCore 0:
  38.9 62.5 all-gather.4
  103.6 67.3 all-gather.6
  173.1 69.0 all-gather.8
  244.6 67.2 all-gather.10
where the time goes:
time: 399 us; the launch traced here: 396 us
  waiting for transfers between devices  114 us (29%)
  blocking collectives  94.7 us (24%)
  local copies, waits for them, and re-layouts  73.4 us (18%)
  starting transfers between devices  45.2 us (11%)
  between operations  30.7 us (8%)
  matrix products  22.9 us (6%)
  other arithmetic  13.8 us (3%)
    all_gather x1, waiting for transfers between devices, per_device(): lax.all_gather(head_grads, 'blk', axis=0, tiled=True)  53.8 us
    all_gather x1, blocking collectives, per_device(): lax.all_gather(head_sums, 'blk', axis=0, tiled=True)  34.3 us
    all_gather x1, blocking collectives, per_device(): lax.all_gather(head_mass, 'blk', axis=0, tiled=True)  30.5 us
    all_to_all x1, blocking collectives, per_device(): lax.all_to_all(jnp.repeat(separate_heads(key_matrix, KEY_VALUE_HEADS), gr...  29.9 us
    unnamed x274, local copies, waits for them, and re-layouts  20.7 us
    all_to_all x1, waiting for transfers between devices, per_device(): lax.all_to_all(jnp.repeat(separate_heads(value_matrix, KEY_VALUE_HEADS),...  15 us
    all_to_all x1, waiting for transfers between devices, per_device(): lax.all_to_all((softmax_scale * key_acc).astype(jnp.bfloat16), 'uly', spl...  13.9 us
    all_to_all x1, waiting for transfers between devices, per_device(): lax.all_to_all(separate_heads(output_grad, QUERY_HEADS), 'uly', split_axi...  13 us
  transfers between devices with their start and end apart: 11, of which 6 were waited for; matrix products, arithmetic and copies ran while one was open for 25% of the time, Pallas kernels for 0%

commit v1 on v0

v1 whole, which is shorter than its diff:
```python
import functools
import math

import jax
import jax.numpy as jnp
from jax import lax
from jax.experimental import pallas as pl
from jax.experimental.pallas import tpu as pltpu
from jax.sharding import PartitionSpec as P

GROUPS = 4
WIDTH = 4
HEAD = 128
ROWS = 128
RUN = 8
STRETCHES = 64
SEQUENCE = STRETCHES * RUN * ROWS
TILE = 16
TILES = ROWS // TILE
NEGATIVE = -1e30
MESH = pl.DeviceIdType.MESH
F32 = jnp.float32
BF16 = jnp.bfloat16


def device_of(stretch, z):
    return (lax.div(stretch, 2), lax.rem(stretch, 2) * RUN + z)


def router_of(group, tile):
    y = lax.div(tile, 2)
    return y * 8 + lax.rem(tile, 2) * 4 + lax.rem(group - y + 8, 4)


def routed_by(stretch):
    y = lax.div(stretch, 8)
    tile = y * 2 + lax.rem(lax.div(stretch, 4), 2)
    return lax.rem(stretch + y, 4), lax.div(tile, TILES), lax.rem(tile, TILES)


def rows_of(tile):
    return pl.ds(pl.multiple_of(tile * TILE, TILE), TILE)


def columns_of(group):
    return pl.ds(pl.multiple_of(group * HEAD, HEAD), HEAD)


def as_column(row):
    n = row.shape[1]
    same = lax.broadcasted_iota(jnp.int32, (n, n), 0) == lax.broadcasted_iota(jnp.int32, (n, n), 1)
    spread = jnp.broadcast_to(row.astype(F32), (n, n))
    return jnp.sum(jnp.where(same, spread, 0.0), axis=1, keepdims=True)


def number_in(table, line, stretch):
    return jnp.clip(table[line, stretch], 0, STRETCHES - 1)


def wait_bytes(ref, sem):
    pltpu.make_async_copy(ref, ref, sem).wait()


def kernel(
    order, document_ids, query, key, value, layer_output, output_grad,
    dq, dk, dv,
    documents, q, o, do, k, v, own, before, back, returned, arrived, routed, arrived_back,
    routed_back, table, table_smem,
    in_sem, table_sem, kv_send, kv_recv, route_sem, route_send, back_send,
    route_back_sem, route_back_send, back_recv,
):
    blk, uly = lax.axis_index("blk"), lax.axis_index("uly")
    z = lax.rem(uly, RUN)
    me = blk * 2 + lax.div(uly, RUN)
    first, last = z == 0, z == RUN - 1
    group_here, kind_here, tile_here = routed_by(me)
    softmax_scale = 1.0 / math.sqrt(HEAD)

    loads = [
        pltpu.make_async_copy(source, target, in_sem.at[i])
        for i, (source, target) in enumerate(
            (
                (document_ids, documents),
                (key, k),
                (query, q),
                (value, v),
                (output_grad, do),
                (layer_output, o),
            )
        )
    ]
    for load in loads:
        load.start()

    barrier = pltpu.get_barrier_semaphore()

    def greet(stretch, at):
        pl.semaphore_signal(barrier, inc=1, device_id=device_of(stretch, at), device_id_type=MESH)

    @pl.when(first)
    def _():
        def to_last(i, carry):
            greet(i, RUN - 1)
            return carry

        def to_first(i, carry):
            greet(lax.rem(me + 1 + i, STRETCHES), 0)
            return carry

        lax.fori_loop(0, STRETCHES, to_last, 0)
        lax.fori_loop(0, STRETCHES - 1, to_first, 0)
        greet(me, 1)
        pl.semaphore_wait(barrier, STRETCHES)

    @pl.when(last)
    def _():
        greet(me, RUN - 2)
        pl.semaphore_wait(barrier, STRETCHES + 1)

    @pl.when(jnp.logical_not(first | last))
    def _():
        greet(me, z - 1)
        greet(me, z + 1)
        pl.semaphore_wait(barrier, 2)

    @pl.when(jnp.logical_not(last))
    def _():
        for group in range(GROUPS):
            for kind, source in enumerate((key, value)):
                pltpu.make_async_remote_copy(
                    source.at[:, pl.ds(group * HEAD, HEAD)],
                    before.at[group, kind],
                    kv_send,
                    kv_recv.at[group],
                    device_id=device_of(me, z + 1),
                    device_id_type=MESH,
                ).start()

    @pl.when(last)
    def _():
        def send(i, carry):
            group, tile = lax.div(i, TILES), lax.rem(i, TILES)
            for kind, source in enumerate((key, value)):
                pltpu.make_async_remote_copy(
                    source.at[rows_of(tile), columns_of(group)],
                    arrived.at[me],
                    kv_send,
                    route_sem,
                    device_id=device_of(router_of(group, kind * TILES + tile), 0),
                    device_id_type=MESH,
                ).start()
            return carry

        lax.fori_loop(0, GROUPS * TILES, send, 0)

    @pl.when(first | last)
    def _():
        lane = lax.broadcasted_iota(jnp.int32, (1, HEAD), 1)
        row = jnp.zeros((1, HEAD), jnp.int32)
        for stretch in range(STRETCHES):
            row = jnp.where(lane == stretch, order[stretch], row)
        previous = jnp.where(row == 0, STRETCHES - 1, row - 1)
        following = jnp.where(row == STRETCHES - 1, 0, row + 1)
        for i, wanted in enumerate((previous, following)):
            found = jnp.zeros((1, HEAD), jnp.int32)
            for stretch in range(STRETCHES):
                found = jnp.where(wanted == order[stretch], stretch, found)
            table[i : i + 1, :] = found
        copy = pltpu.make_async_copy(table, table_smem, table_sem)
        copy.start()
        copy.wait()

    loads[0].wait()
    place = order[me] * RUN + z
    query_document = documents[pl.ds(place, 1), :]
    before_document = documents[pl.ds(jnp.maximum(place - 1, 0), 1), :]
    before_document = jnp.where(place == 0, -1, before_document)
    down = lax.broadcasted_iota(jnp.int32, (ROWS, ROWS), 0)
    across = lax.broadcasted_iota(jnp.int32, (ROWS, ROWS), 1)
    wanted = query_document.astype(F32)
    before_bias = jnp.where(as_column(before_document) == wanted, 0.0, NEGATIVE)
    own_bias = jnp.where(
        (as_column(query_document) == wanted) & (down <= across), 0.0, NEGATIVE
    )
    bias = jnp.concatenate([before_bias, own_bias], axis=0)
    bias = jnp.concatenate([bias] * WIDTH, axis=1)

    @pl.when(first)
    def _():
        wait_bytes(arrived, route_sem)

        def pass_on(i, carry):
            stretch = lax.rem(me + 1 + i, STRETCHES)
            routed[stretch] = arrived[number_in(table_smem, 0, stretch)]
            pltpu.make_async_remote_copy(
                routed.at[stretch],
                before.at[group_here, kind_here, rows_of(tile_here)],
                route_send,
                kv_recv.at[group_here],
                device_id=device_of(stretch, 0),
                device_id_type=MESH,
            ).start()
            return carry

        lax.fori_loop(0, STRETCHES - 1, pass_on, 0)
        routed[me] = arrived[number_in(table_smem, 0, me)]
        pltpu.make_async_copy(
            routed.at[me],
            before.at[group_here, kind_here, rows_of(tile_here)],
            kv_recv.at[group_here],
        ).start()

    for load in loads[1:]:
        load.wait()

    contract_features = (((1,), (1,)), ((), ()))
    contract_rows = (((0,), (0,)), ((), ()))
    minus_ones = jnp.full((2 * ROWS, HEAD), -1.0, BF16)
    for group in range(GROUPS):
        wait_bytes(before.at[group], kv_recv.at[group])
        columns = slice(group * HEAD, (group + 1) * HEAD)

        def heads(tensor):
            return jnp.concatenate(
                [
                    tensor[:, (group * WIDTH + h) * HEAD : (group * WIDTH + h + 1) * HEAD]
                    for h in range(WIDTH)
                ],
                axis=0,
            )

        keys = jnp.concatenate([before[group, 0], k[:, columns]], axis=0)
        values = jnp.concatenate([before[group, 1], v[:, columns]], axis=0)
        queries, grads = heads(q), heads(do)
        products = (grads.astype(F32) * heads(o).astype(F32)).astype(BF16)
        scores = lax.dot_general(keys, queries, contract_features, preferred_element_type=F32)
        scores = scores * (softmax_scale * math.log2(math.e)) + bias
        weights = jnp.exp2(scores - jnp.max(scores, axis=0, keepdims=True))
        probability = weights * (1.0 / jnp.sum(weights, axis=0, keepdims=True))
        centred = lax.dot_general(
            jnp.concatenate([values, minus_ones], axis=1),
            jnp.concatenate([grads, products], axis=1),
            contract_features,
            preferred_element_type=F32,
        )
        slopes = (probability * centred).astype(BF16)
        key_part = softmax_scale * jnp.dot(slopes, queries, preferred_element_type=F32)
        value_part = jnp.dot(probability.astype(BF16), grads, preferred_element_type=F32)
        back[group, 0] = key_part[:ROWS].astype(BF16)
        back[group, 1] = value_part[:ROWS].astype(BF16)

        @pl.when(first)
        def _():
            def send(tile, carry):
                for kind in range(2):
                    pltpu.make_async_remote_copy(
                        back.at[group, kind, rows_of(tile)],
                        arrived_back.at[me],
                        back_send,
                        route_back_sem,
                        device_id=device_of(router_of(group, kind * TILES + tile), RUN - 1),
                        device_id_type=MESH,
                    ).start()
                return carry

            lax.fori_loop(0, TILES, send, 0)

        @pl.when(jnp.logical_not(first))
        def _():
            pltpu.make_async_remote_copy(
                back.at[group],
                returned.at[group],
                back_send,
                back_recv.at[group],
                device_id=device_of(me, z - 1),
                device_id_type=MESH,
            ).start()

        own[group, 0] = key_part[ROWS:]
        own[group, 1] = value_part[ROWS:]
        query_part = softmax_scale * lax.dot_general(
            slopes, keys, contract_rows, preferred_element_type=F32
        )
        for h in range(WIDTH):
            head = group * WIDTH + h
            dq[:, head * HEAD : (head + 1) * HEAD] = query_part[h * ROWS : (h + 1) * ROWS].astype(
                BF16
            )

    @pl.when(last)
    def _():
        wait_bytes(arrived_back, route_back_sem)

        def pass_on(i, carry):
            stretch = lax.rem(me + 1 + i, STRETCHES)
            routed_back[stretch] = arrived_back[number_in(table_smem, 1, stretch)]
            pltpu.make_async_remote_copy(
                routed_back.at[stretch],
                returned.at[group_here, kind_here, rows_of(tile_here)],
                route_back_send,
                back_recv.at[group_here],
                device_id=device_of(stretch, RUN - 1),
                device_id_type=MESH,
            ).start()
            return carry

        lax.fori_loop(0, STRETCHES - 1, pass_on, 0)
        routed_back[me] = arrived_back[number_in(table_smem, 1, me)]
        pltpu.make_async_copy(
            routed_back.at[me],
            returned.at[group_here, kind_here, rows_of(tile_here)],
            back_recv.at[group_here],
        ).start()

    for group in range(GROUPS):
        wait_bytes(returned.at[group], back_recv.at[group])
        columns = slice(group * HEAD, (group + 1) * HEAD)
        dk[:, columns] = (own[group, 0] + returned[group, 0].astype(F32)).astype(BF16)
        dv[:, columns] = (own[group, 1] + returned[group, 1].astype(F32)).astype(BF16)

    wait_bytes(before, kv_send)
    wait_bytes(back, back_send)

    @pl.when(first)
    def _():
        wait_bytes(routed.at[pl.ds(0, STRETCHES - 1)], route_send)

    @pl.when(last)
    def _():
        wait_bytes(routed_back.at[pl.ds(0, STRETCHES - 1)], route_back_send)


def per_device(
    query_states, key_matrix, value_matrix, layer_output, output_grad, stretch_order, document_ids
):
    vmem = pl.BlockSpec(memory_space=pltpu.VMEM)
    hbm = pl.BlockSpec(memory_space=pltpu.HBM)
    wide, narrow = query_states.shape, key_matrix.shape
    halo = (GROUPS, 2, ROWS, HEAD)
    routes = (STRETCHES, TILE, HEAD)
    dma = pltpu.SemaphoreType.DMA
    return pl.pallas_call(
        kernel,
        out_shape=[
            jax.ShapeDtypeStruct(wide, BF16),
            jax.ShapeDtypeStruct(narrow, BF16),
            jax.ShapeDtypeStruct(narrow, BF16),
        ],
        in_specs=[pl.BlockSpec(memory_space=pltpu.SMEM)] + [hbm] * 6,
        out_specs=[vmem] * 3,
        scratch_shapes=[
            pltpu.VMEM((SEQUENCE // ROWS, ROWS), jnp.int32),
            pltpu.VMEM(wide, BF16),
            pltpu.VMEM(wide, BF16),
            pltpu.VMEM(wide, BF16),
            pltpu.VMEM(narrow, BF16),
            pltpu.VMEM(narrow, BF16),
            pltpu.VMEM(halo, F32),
            pltpu.VMEM(halo, BF16),
            pltpu.VMEM(halo, BF16),
            pltpu.VMEM(halo, BF16),
            pltpu.VMEM(routes, BF16),
            pltpu.VMEM(routes, BF16),
            pltpu.VMEM(routes, BF16),
            pltpu.VMEM(routes, BF16),
            pltpu.VMEM((8, 128), jnp.int32),
            pltpu.SMEM((8, 128), jnp.int32),
            dma((6,)),
            dma(()),
            dma(()),
            dma((GROUPS,)),
            dma(()),
            dma(()),
            dma(()),
            dma(()),
            dma(()),
            dma((GROUPS,)),
        ],
        compiler_params=pltpu.CompilerParams(
            collective_id=0, has_side_effects=True, vmem_limit_bytes=40 * 2**20
        ),
        cost_estimate=pl.CostEstimate(
            flops=671_000_000, bytes_accessed=2_700_000, transcendentals=524_288
        ),
    )(
        stretch_order,
        *(
            pltpu.with_memory_space_constraint(operand, pltpu.HBM)
            for operand in (
                document_ids.reshape(-1, ROWS),
                query_states,
                key_matrix,
                value_matrix,
                layer_output,
                output_grad,
            )
        ),
    )


def solution(mesh):
    rows = P(("blk", "uly"), None)
    return jax.shard_map(
        per_device,
        mesh=mesh,
        in_specs=(rows, rows, rows, rows, rows, P(), P()),
        out_specs=(rows, rows, rows),
        check_vma=False,
    )
```

time: 399 us -> 45.7 us (0.11)
  the two profiles are of different devices: /device:TPU:8 before, /device:TPU:449 now
where the time goes in v1:
time: 45.7 us; the launch traced here: 45.6 us
  Pallas kernels  42.2 us (92%)
  local copies, waits for them, and re-layouts  2.75 us (6%)
  between operations  0.65 us (1%)
    pallas_call x1, Pallas kernels, per_device(): pl.pallas_call(kernel, out_shape=[jax.ShapeDtypeStruct(wide, BF16), jax.S...  42.2 us
    unnamed x5, local copies, waits for them, and re-layouts  2.75 us

profile of v1, /device:TPU:449, one launch (start us, length us, event | category | flops | bytes accessed | tf_op | source)
XLA Modules:
  0.0 45.6 jit_solution(4711226778730153803)
XLA Ops:
  0.6 0.0 copy-start
  0.6 0.6 %copy-done = s32[64]{0:T(128)S(1)} copy-done((s32[64]{0:T(128)S(1)}, s32[64]{0:T(128)}, u32[]{:S(2)}) %copy-start) | copy-done | bytes 280
  1.3 42.2 %shard_map.94 = (bf16[128,2048]{1,0:T(8,128)(2,1)S(1)}, bf16[128,512]{1,0:T(8,128)(2,1)S(1)}, bf16[128,512]{1,0:T(8,128)(2,1)S(1)}) custom-call(s32[64]{0:T(128)S(1)} %copy-done, s32[512,128]{1,0:T(8,128)} %bitcast.1, bf16[128,2048]{1,0:T(8,128)(2,1)} %query.1, bf16[128,512]{1,0:T(8,128)(2,1)} %key.1, bf16[128,512]{1,0:T(8,128)(2,1)} %value.1, ...), custom_call_target="tpu_custom_call" | custom-call | flops 671000000 | bytes 2700000 | tf_op jit(solution)/shard_map/pallas_call | solution.py:342
  43.5 0.8 %copy.13 = bf16[128,2048]{1,0:T(8,128)(2,1)} copy(bf16[128,2048]{1,0:T(8,128)(2,1)S(1)} %get-tuple-element.6) | data formatting | bytes 1048576
  44.3 0.7 %copy.14 = bf16[128,512]{1,0:T(8,128)(2,1)} copy(bf16[128,512]{1,0:T(8,128)(2,1)S(1)} %get-tuple-element.7) | data formatting | bytes 262144
  44.9 0.7 %copy.15 = bf16[128,512]{1,0:T(8,128)(2,1)} copy(bf16[128,512]{1,0:T(8,128)(2,1)S(1)} %get-tuple-element.8) | data formatting | bytes 262144
Async XLA Ops:
  0.6 0.7 %copy-start = (s32[64]{0:T(128)S(1)}, s32[64]{0:T(128)}, u32[]{:S(2)}) copy-start(s32[64]{0:T(128)} %order.1) | copy-start | bytes 772

commit v2 on v1

--- a/solution.py
+++ b/solution.py
@@ -17,6 +17,7 @@
 SEQUENCE = STRETCHES * RUN * ROWS
 TILE = 16
 TILES = ROWS // TILE
+Y_STEPS = (4, 1, 3, 7, 5, 2, 6, 0)
 NEGATIVE = -1e30
 MESH = pl.DeviceIdType.MESH
 F32 = jnp.float32
@@ -27,15 +28,38 @@
     return (lax.div(stretch, 2), lax.rem(stretch, 2) * RUN + z)
 
 
-def router_of(group, tile):
-    y = lax.div(tile, 2)
-    return y * 8 + lax.rem(tile, 2) * 4 + lax.rem(group - y + 8, 4)
+def place_of(stretch):
+    x = 2 * lax.rem(stretch, 2) + lax.rem(lax.div(stretch, 4), 2)
+    return lax.div(stretch, 8), x, lax.rem(lax.div(stretch, 2), 2)
 
 
 def routed_by(stretch):
-    y = lax.div(stretch, 8)
-    tile = y * 2 + lax.rem(lax.div(stretch, 4), 2)
-    return lax.rem(stretch + y, 4), lax.div(tile, TILES), lax.rem(tile, TILES)
+    y, x, core = place_of(stretch)
+    return core * 2 + lax.rem(lax.div(x, 2) + y, 2), lax.rem(x, 2), y
+
+
+def for_core(me, core, visit, but_own=False):
+    y, x, _ = place_of(me)
+
+    def at(y_step, x_step):
+        there_y, there_x = lax.rem(y + y_step, 8), lax.rem(x + x_step, 4)
+        visit(there_y * 8 + lax.rem(there_x, 2) * 4 + core * 2 + lax.div(there_x, 2))
+
+    def column(i, carry):
+        x_step = jnp.where(i == 0, 2, jnp.where(i == 1, 1, 3))
+        for y_step in Y_STEPS:
+            at(y_step, x_step)
+        return carry
+
+    lax.fori_loop(0, 3, column, 0)
+    for y_step in Y_STEPS[:-1] if but_own else Y_STEPS:
+        at(y_step, 0)
+
+
+def for_others(me, visit):
+    core = place_of(me)[2]
+    for_core(me, 1 - core, visit)
+    for_core(me, core, visit, but_own=True)
 
 
 def rows_of(tile):
@@ -62,9 +86,9 @@
 
 
 def kernel(
-    order, document_ids, query, key, value, layer_output, output_grad,
+    stretch_order, document_ids, query, key, value, layer_output, output_grad,
     dq, dk, dv,
-    documents, q, o, do, k, v, own, before, back, returned, arrived, routed, arrived_back,
+    order, documents, q, o, do, k, v, with_products, scores, centred, inverses, slopes, own, before, back, returned, arrived, routed, arrived_back,
     routed_back, table, table_smem,
     in_sem, table_sem, kv_send, kv_recv, route_sem, route_send, back_send,
     route_back_sem, route_back_send, back_recv,
@@ -80,6 +104,7 @@
         pltpu.make_async_copy(source, target, in_sem.at[i])
         for i, (source, target) in enumerate(
             (
+                (stretch_order, order),
                 (document_ids, documents),
                 (key, k),
                 (query, q),
@@ -99,16 +124,9 @@
 
     @pl.when(first)
     def _():
-        def to_last(i, carry):
-            greet(i, RUN - 1)
-            return carry
-
-        def to_first(i, carry):
-            greet(lax.rem(me + 1 + i, STRETCHES), 0)
-            return carry
-
-        lax.fori_loop(0, STRETCHES, to_last, 0)
-        lax.fori_loop(0, STRETCHES - 1, to_first, 0)
+        for core in range(2):
+            for_core(me, core, lambda stretch: greet(stretch, RUN - 1))
+        for_others(me, lambda stretch: greet(stretch, 0))
         greet(me, 1)
         pl.semaphore_wait(barrier, STRETCHES)
 
@@ -138,20 +156,26 @@
 
     @pl.when(last)
     def _():
-        def send(i, carry):
-            group, tile = lax.div(i, TILES), lax.rem(i, TILES)
-            for kind, source in enumerate((key, value)):
-                pltpu.make_async_remote_copy(
-                    source.at[rows_of(tile), columns_of(group)],
-                    arrived.at[me],
-                    kv_send,
-                    route_sem,
-                    device_id=device_of(router_of(group, kind * TILES + tile), 0),
-                    device_id_type=MESH,
-                ).start()
-            return carry
-
-        lax.fori_loop(0, GROUPS * TILES, send, 0)
+        def send(stretch):
+            group, kind, tile = routed_by(stretch)
+            for i, source in enumerate((key, value)):
+
+                @pl.when(kind == i)
+                def _():
+                    pltpu.make_async_remote_copy(
+                        source.at[rows_of(tile), columns_of(group)],
+                        arrived.at[me],
+                        kv_send,
+                        route_sem,
+                        device_id=device_of(stretch, 0),
+                        device_id_type=MESH,
+                    ).start()
+
+        for core in range(2):
+            for_core(me, core, send)
+
+    loads[0].wait()
+    loads[1].wait()
 
     @pl.when(first | last)
     def _():
@@ -170,7 +194,6 @@
         copy.start()
         copy.wait()
 
-    loads[0].wait()
     place = order[me] * RUN + z
     query_document = documents[pl.ds(place, 1), :]
     before_document = documents[pl.ds(jnp.maximum(place - 1, 0), 1), :]
@@ -182,15 +205,14 @@
     own_bias = jnp.where(
         (as_column(query_document) == wanted) & (down <= across), 0.0, NEGATIVE
     )
-    bias = jnp.concatenate([before_bias, own_bias], axis=0)
-    bias = jnp.concatenate([bias] * WIDTH, axis=1)
+    before_bias = jnp.concatenate([before_bias] * WIDTH, axis=1)
+    own_bias = jnp.concatenate([own_bias] * WIDTH, axis=1)
 
     @pl.when(first)
     def _():
         wait_bytes(arrived, route_sem)
 
-        def pass_on(i, carry):
-            stretch = lax.rem(me + 1 + i, STRETCHES)
+        def pass_on(stretch):
             routed[stretch] = arrived[number_in(table_smem, 0, stretch)]
             pltpu.make_async_remote_copy(
                 routed.at[stretch],
@@ -200,9 +222,8 @@
                 device_id=device_of(stretch, 0),
                 device_id_type=MESH,
             ).start()
-            return carry
-
-        lax.fori_loop(0, STRETCHES - 1, pass_on, 0)
+
+        for_others(me, pass_on)
         routed[me] = arrived[number_in(table_smem, 0, me)]
         pltpu.make_async_copy(
             routed.at[me],
@@ -210,60 +231,70 @@
             kv_recv.at[group_here],
         ).start()
 
-    for load in loads[1:]:
+    for load in loads[2:]:
         load.wait()
 
     contract_features = (((1,), (1,)), ((), ()))
     contract_rows = (((0,), (0,)), ((), ()))
-    minus_ones = jnp.full((2 * ROWS, HEAD), -1.0, BF16)
+    minus_ones = jnp.full((ROWS, HEAD), -1.0, BF16)
+    scale_2 = softmax_scale * math.log2(math.e)
+
+    def heads(tensor, group):
+        return jnp.concatenate(
+            [
+                tensor[:, (group * WIDTH + h) * HEAD : (group * WIDTH + h + 1) * HEAD]
+                for h in range(WIDTH)
+            ],
+            axis=0,
+        )
+
+    def scores_of(keys, group, bias):
+        product = lax.dot_general(
+            keys, heads(q, group), contract_features, preferred_element_type=F32
+        )
+        return product * scale_2 + bias
+
+    def centred_of(values, group):
+        return lax.dot_general(
+            jnp.concatenate([values, minus_ones], axis=1),
+            with_products[group],
+            contract_features,
+            preferred_element_type=F32,
+        )
+
+    for group in range(GROUPS):
+        columns = slice(group * HEAD, (group + 1) * HEAD)
+        grads = heads(do, group)
+        products = (grads.astype(F32) * heads(o, group).astype(F32)).astype(BF16)
+        with_products[group] = jnp.concatenate([grads, products], axis=1)
+        scores[group] = scores_of(k[:, columns], group, own_bias)
+        centred[group] = centred_of(v[:, columns], group)
+
     for group in range(GROUPS):
         wait_bytes(before.at[group], kv_recv.at[group])
-        columns = slice(group * HEAD, (group + 1) * HEAD)
-
-        def heads(tensor):
-            return jnp.concatenate(
-                [
-                    tensor[:, (group * WIDTH + h) * HEAD : (group * WIDTH + h + 1) * HEAD]
-                    for h in range(WIDTH)
-                ],
-                axis=0,
-            )
-
-        keys = jnp.concatenate([before[group, 0], k[:, columns]], axis=0)
-        values = jnp.concatenate([before[group, 1], v[:, columns]], axis=0)
-        queries, grads = heads(q), heads(do)
-        products = (grads.astype(F32) * heads(o).astype(F32)).astype(BF16)
-        scores = lax.dot_general(keys, queries, contract_features, preferred_element_type=F32)
-        scores = scores * (softmax_scale * math.log2(math.e)) + bias
-        weights = jnp.exp2(scores - jnp.max(scores, axis=0, keepdims=True))
-        probability = weights * (1.0 / jnp.sum(weights, axis=0, keepdims=True))
-        centred = lax.dot_general(
-            jnp.concatenate([values, minus_ones], axis=1),
-            jnp.concatenate([grads, products], axis=1),
-            contract_features,
-            preferred_element_type=F32,
-        )
-        slopes = (probability * centred).astype(BF16)
-        key_part = softmax_scale * jnp.dot(slopes, queries, preferred_element_type=F32)
-        value_part = jnp.dot(probability.astype(BF16), grads, preferred_element_type=F32)
-        back[group, 0] = key_part[:ROWS].astype(BF16)
-        back[group, 1] = value_part[:ROWS].astype(BF16)
-
-        @pl.when(first)
-        def _():
-            def send(tile, carry):
-                for kind in range(2):
-                    pltpu.make_async_remote_copy(
-                        back.at[group, kind, rows_of(tile)],
-                        arrived_back.at[me],
-                        back_send,
-                        route_back_sem,
-                        device_id=device_of(router_of(group, kind * TILES + tile), RUN - 1),
-                        device_id_type=MESH,
-                    ).start()
-                return carry
-
-            lax.fori_loop(0, TILES, send, 0)
+        before_scores = scores_of(before[group, 0], group, before_bias)
+        own_scores = scores[group]
+        peak = jnp.maximum(
+            jnp.max(before_scores, axis=0, keepdims=True),
+            jnp.max(own_scores, axis=0, keepdims=True),
+        )
+        before_weights = jnp.exp2(before_scores - peak)
+        own_weights = jnp.exp2(own_scores - peak)
+        scores[group] = own_weights
+        inverse = 1.0 / (
+            jnp.sum(before_weights, axis=0, keepdims=True)
+            + jnp.sum(own_weights, axis=0, keepdims=True)
+        )
+        inverses[group : group + 1, :] = inverse
+        probability = before_weights * inverse
+        slope = (probability * centred_of(before[group, 1], group)).astype(BF16)
+        slopes[group, :ROWS] = slope
+        back[group, 0] = (
+            softmax_scale * jnp.dot(slope, heads(q, group), preferred_element_type=F32)
+        ).astype(BF16)
+        back[group, 1] = jnp.dot(
+            probability.astype(BF16), heads(do, group), preferred_element_type=F32
+        ).astype(BF16)
 
         @pl.when(jnp.logical_not(first))
         def _():
@@ -276,10 +307,35 @@
                 device_id_type=MESH,
             ).start()
 
-        own[group, 0] = key_part[ROWS:]
-        own[group, 1] = value_part[ROWS:]
+        if group % 2 == 1:
+
+            @pl.when(first)
+            def _():
+                def send(stretch):
+                    there, kind, tile = routed_by(stretch)
+                    pltpu.make_async_remote_copy(
+                        back.at[there, kind, rows_of(tile)],
+                        arrived_back.at[me],
+                        back_send,
+                        route_back_sem,
+                        device_id=device_of(stretch, RUN - 1),
+                        device_id_type=MESH,
+                    ).start()
+
+                for_core(me, group // 2, send)
+
+    for group in range(GROUPS):
+        columns = slice(group * HEAD, (group + 1) * HEAD)
+        probability = scores[group] * inverses[group : group + 1, :]
+        slope = (probability * centred[group]).astype(BF16)
+        slopes[group, ROWS:] = slope
+        own[group, 0] = softmax_scale * jnp.dot(slope, heads(q, group), preferred_element_type=F32)
+        own[group, 1] = jnp.dot(
+            probability.astype(BF16), heads(do, group), preferred_element_type=F32
+        )
+        keys = jnp.concatenate([before[group, 0], k[:, columns]], axis=0)
         query_part = softmax_scale * lax.dot_general(
-            slopes, keys, contract_rows, preferred_element_type=F32
+            slopes[group], keys, contract_rows, preferred_element_type=F32
         )
         for h in range(WIDTH):
             head = group * WIDTH + h
@@ -291,8 +347,7 @@
     def _():
         wait_bytes(arrived_back, route_back_sem)
 
-        def pass_on(i, carry):
-            stretch = lax.rem(me + 1 + i, STRETCHES)
+        def pass_on(stretch):
             routed_back[stretch] = arrived_back[number_in(table_smem, 1, stretch)]
             pltpu.make_async_remote_copy(
                 routed_back.at[stretch],
@@ -302,9 +357,8 @@
                 device_id=device_of(stretch, RUN - 1),
                 device_id_type=MESH,
             ).start()
-            return carry
-
-        lax.fori_loop(0, STRETCHES - 1, pass_on, 0)
+
+        for_others(me, pass_on)
         routed_back[me] = arrived_back[number_in(table_smem, 1, me)]
         pltpu.make_async_copy(
             routed_back.at[me],
@@ -328,6 +382,17 @@
     @pl.when(last)
     def _():
         wait_bytes(routed_back.at[pl.ds(0, STRETCHES - 1)], route_back_send)
+
+
+def store(dq, dk, dv, query_grad, key_grad, value_grad, sem):
+    copies = [
+        pltpu.make_async_copy(source, target, sem.at[i])
+        for i, (source, target) in enumerate(((dq, query_grad), (dk, key_grad), (dv, value_grad)))
+    ]
+    for copy in copies:
+        copy.start()
+    for copy in copies:
+        copy.wait()
 
 
 def per_device(
@@ -339,22 +404,28 @@
     halo = (GROUPS, 2, ROWS, HEAD)
     routes = (STRETCHES, TILE, HEAD)
     dma = pltpu.SemaphoreType.DMA
-    return pl.pallas_call(
+    grads = pl.pallas_call(
         kernel,
         out_shape=[
-            jax.ShapeDtypeStruct(wide, BF16),
-            jax.ShapeDtypeStruct(narrow, BF16),
-            jax.ShapeDtypeStruct(narrow, BF16),
+            pltpu.VMEM(wide, BF16),
+            pltpu.VMEM(narrow, BF16),
+            pltpu.VMEM(narrow, BF16),
         ],
-        in_specs=[pl.BlockSpec(memory_space=pltpu.SMEM)] + [hbm] * 6,
+        in_specs=[hbm] * 7,
         out_specs=[vmem] * 3,
         scratch_shapes=[
+            pltpu.SMEM((STRETCHES,), jnp.int32),
             pltpu.VMEM((SEQUENCE // ROWS, ROWS), jnp.int32),
             pltpu.VMEM(wide, BF16),
             pltpu.VMEM(wide, BF16),
             pltpu.VMEM(wide, BF16),
             pltpu.VMEM(narrow, BF16),
             pltpu.VMEM(narrow, BF16),
+            pltpu.VMEM((GROUPS, WIDTH * ROWS, 2 * HEAD), BF16),
+            pltpu.VMEM((GROUPS, ROWS, WIDTH * ROWS), F32),
+            pltpu.VMEM((GROUPS, ROWS, WIDTH * ROWS), F32),
+            pltpu.VMEM((8, WIDTH * ROWS), F32),
+            pltpu.VMEM((GROUPS, 2 * ROWS, WIDTH * ROWS), BF16),
             pltpu.VMEM(halo, F32),
             pltpu.VMEM(halo, BF16),
             pltpu.VMEM(halo, BF16),
@@ -365,7 +436,7 @@
             pltpu.VMEM(routes, BF16),
             pltpu.VMEM((8, 128), jnp.int32),
             pltpu.SMEM((8, 128), jnp.int32),
-            dma((6,)),
+            dma((7,)),
             dma(()),
             dma(()),
             dma((GROUPS,)),
@@ -383,10 +454,10 @@
             flops=671_000_000, bytes_accessed=2_700_000, transcendentals=524_288
         ),
     )(
-        stretch_order,
         *(
             pltpu.with_memory_space_constraint(operand, pltpu.HBM)
             for operand in (
+                stretch_order,
                 document_ids.reshape(-1, ROWS),
                 query_states,
                 key_matrix,
@@ -397,6 +468,15 @@
         ),
     )
 
+    return pl.pallas_call(
+        store,
+        out_shape=[jax.ShapeDtypeStruct(grad.shape, BF16) for grad in grads],
+        in_specs=[vmem] * 3,
+        out_specs=[pl.BlockSpec(memory_space=pl.ANY)] * 3,
+        scratch_shapes=[dma((3,))],
+        compiler_params=pltpu.CompilerParams(vmem_limit_bytes=40 * 2**20),
+    )(*[grad for grad in grads])
+
 
 def solution(mesh):
     rows = P(("blk", "uly"), None)

time: 45.7 us -> 41.9 us (0.917)
  local copies, waits for them, and re-layouts: 2.75 us -> 0 us
  Pallas kernels: 42.2 us -> 41.1 us
    unnamed x5 -> x0, local copies, waits for them, and re-layouts: 2.75 us -> none
    pallas_call x1 -> x2, Pallas kernels: 42.2 us -> 41.1 us  [the longest x1 40.2 us: per_device(): pl.pallas_call(kernel, out_shape=[pltpu.VMEM(wide, BF16), pltpu.VMEM(narr...]
where the time goes in v2:
time: 41.9 us; the launch traced here: 41.8 us
  Pallas kernels  41.1 us (98%)
  between operations  0.64 us (2%)
    pallas_call x1, Pallas kernels, per_device(): pl.pallas_call(kernel, out_shape=[pltpu.VMEM(wide, BF16), pltpu.VMEM(narr...  40.2 us
    pallas_call x1, Pallas kernels, per_device(): pl.pallas_call(store, out_shape=[jax.ShapeDtypeStruct(grad.shape, BF16) f...  0.9 us

profile of v2, /device:TPU:449, one launch (start us, length us, event | category | flops | bytes accessed | tf_op | source)
XLA Modules:
  0.0 41.8 jit_solution(14399451541714143073)
XLA Ops:
  0.6 40.2 %shard_map.94 = (bf16[128,2048]{1,0:T(8,128)(2,1)S(1)}, bf16[128,512]{1,0:T(8,128)(2,1)S(1)}, bf16[128,512]{1,0:T(8,128)(2,1)S(1)}) custom-call(s32[64]{0:T(128)} %stretch_order.1, s32[512,128]{1,0:T(8,128)} %bitcast.1, bf16[128,2048]{1,0:T(8,128)(2,1)} %query.1, bf16[128,512]{1,0:T(8,128)(2,1)} %key.1, bf16[128,512]{1,0:T(8,128)(2,1)} %value.1, ...), custom_call_target="tpu_custom_call" | custom-call | flops 671000000 | bytes 2700000 | tf_op jit(solution)/shard_map/pallas_call | solution.py:407
  40.9 0.9 %shard_map.95 = (bf16[128,2048]{1,0:T(8,128)(2,1)}, bf16[128,512]{1,0:T(8,128)(2,1)}, bf16[128,512]{1,0:T(8,128)(2,1)}) custom-call(bf16[128,2048]{1,0:T(8,128)(2,1)S(1)} %get-tuple-element.6.dq, bf16[128,512]{1,0:T(8,128)(2,1)S(1)} %get-tuple-element.7.dk, bf16[128,512]{1,0:T(8,128)(2,1)S(1)} %get-tuple-element.8.dv), custom_call_target="tpu_custom_call" | custom-call | tf_op jit(solution)/shard_map/pallas_call | solution.py:471

commit v3 on v2

--- a/solution.py
+++ b/solution.py
@@ -127,19 +127,19 @@
         for core in range(2):
             for_core(me, core, lambda stretch: greet(stretch, RUN - 1))
         for_others(me, lambda stretch: greet(stretch, 0))
-        greet(me, 1)
         pl.semaphore_wait(barrier, STRETCHES)
 
+    @pl.when(jnp.logical_not(first))
+    def _():
+        greet(me, z - 1)
+
     @pl.when(last)
     def _():
-        greet(me, RUN - 2)
-        pl.semaphore_wait(barrier, STRETCHES + 1)
+        pl.semaphore_wait(barrier, STRETCHES)
 
     @pl.when(jnp.logical_not(first | last))
     def _():
-        greet(me, z - 1)
-        greet(me, z + 1)
-        pl.semaphore_wait(barrier, 2)
+        pl.semaphore_wait(barrier, 1)
 
     @pl.when(jnp.logical_not(last))
     def _():
@@ -171,8 +171,9 @@
                         device_id_type=MESH,
                     ).start()
 
-        for core in range(2):
-            for_core(me, core, send)
+        for_core(me, 0, send)
+        wait_bytes(before.at[pl.ds(0, GROUPS // 2)], kv_send)
+        for_core(me, 1, send)
 
     loads[0].wait()
     loads[1].wait()
@@ -372,7 +373,14 @@
         dk[:, columns] = (own[group, 0] + returned[group, 0].astype(F32)).astype(BF16)
         dv[:, columns] = (own[group, 1] + returned[group, 1].astype(F32)).astype(BF16)
 
-    wait_bytes(before, kv_send)
+    @pl.when(last)
+    def _():
+        wait_bytes(before.at[pl.ds(0, GROUPS // 2)], kv_send)
+
+    @pl.when(jnp.logical_not(last))
+    def _():
+        wait_bytes(before, kv_send)
+
     wait_bytes(back, back_send)
 
     @pl.when(first)

time: 41.9 us -> 39.6 us (0.945)
  Pallas kernels: 41.1 us -> 38.8 us
    pallas_call x1, Pallas kernels: 40.2 us -> 37.9 us  [per_device(): pl.pallas_call(kernel, out_shape=[pltpu.VMEM(wide, BF16), pltpu.VMEM(narr...]
where the time goes in v3:
time: 39.6 us; the launch traced here: 39.5 us
  Pallas kernels  38.8 us (98%)
  between operations  0.64 us (2%)
    pallas_call x1, Pallas kernels, per_device(): pl.pallas_call(kernel, out_shape=[pltpu.VMEM(wide, BF16), pltpu.VMEM(narr...  37.9 us
    pallas_call x1, Pallas kernels, per_device(): pl.pallas_call(store, out_shape=[jax.ShapeDtypeStruct(grad.shape, BF16) f...  0.9 us

profile of v3, /device:TPU:449, one launch (start us, length us, event | category | flops | bytes accessed | tf_op | source)
XLA Modules:
  0.0 39.5 jit_solution(8728588591550033239)
XLA Ops:
  0.6 37.9 %shard_map.94 = (bf16[128,2048]{1,0:T(8,128)(2,1)S(1)}, bf16[128,512]{1,0:T(8,128)(2,1)S(1)}, bf16[128,512]{1,0:T(8,128)(2,1)S(1)}) custom-call(s32[64]{0:T(128)} %stretch_order.1, s32[512,128]{1,0:T(8,128)} %bitcast.1, bf16[128,2048]{1,0:T(8,128)(2,1)} %query.1, bf16[128,512]{1,0:T(8,128)(2,1)} %key.1, bf16[128,512]{1,0:T(8,128)(2,1)} %value.1, ...), custom_call_target="tpu_custom_call" | custom-call | flops 671000000 | bytes 2700000 | tf_op jit(solution)/shard_map/pallas_call | solution.py:415
  38.6 0.9 %shard_map.95 = (bf16[128,2048]{1,0:T(8,128)(2,1)}, bf16[128,512]{1,0:T(8,128)(2,1)}, bf16[128,512]{1,0:T(8,128)(2,1)}) custom-call(bf16[128,2048]{1,0:T(8,128)(2,1)S(1)} %get-tuple-element.6.dq, bf16[128,512]{1,0:T(8,128)(2,1)S(1)} %get-tuple-element.7.dk, bf16[128,512]{1,0:T(8,128)(2,1)S(1)} %get-tuple-element.8.dv), custom_call_target="tpu_custom_call" | custom-call | tf_op jit(solution)/shard_map/pallas_call | solution.py:479

commit v4 on v3

--- a/solution.py
+++ b/solution.py
@@ -16,7 +16,6 @@
 STRETCHES = 64
 SEQUENCE = STRETCHES * RUN * ROWS
 TILE = 16
-TILES = ROWS // TILE
 Y_STEPS = (4, 1, 3, 7, 5, 2, 6, 0)
 NEGATIVE = -1e30
 MESH = pl.DeviceIdType.MESH
@@ -60,6 +59,17 @@
     core = place_of(me)[2]
     for_core(me, 1 - core, visit)
     for_core(me, core, visit, but_own=True)
+
+
+def for_others_mixed(me, visit):
+    step = 2 * (2 * place_of(me)[2] - 1)
+
+    def both(stretch):
+        visit(stretch)
+        visit(stretch + step)
+
+    for_core(me, 1 - place_of(me)[2], both, but_own=True)
+    visit(me - step)
 
 
 def rows_of(tile):
@@ -114,8 +124,10 @@
             )
         )
     ]
-    for load in loads:
-        load.start()
+    @pl.when(jnp.logical_not(last))
+    def _():
+        for load in loads:
+            load.start()
 
     barrier = pltpu.get_barrier_semaphore()
 
@@ -174,6 +186,8 @@
         for_core(me, 0, send)
         wait_bytes(before.at[pl.ds(0, GROUPS // 2)], kv_send)
         for_core(me, 1, send)
+        for load in loads:
+            load.start()
 
     loads[0].wait()
     loads[1].wait()
@@ -209,6 +223,45 @@
     before_bias = jnp.concatenate([before_bias] * WIDTH, axis=1)
     own_bias = jnp.concatenate([own_bias] * WIDTH, axis=1)
 
+    for load in loads[2:]:
+        load.wait()
+
+    contract_features = (((1,), (1,)), ((), ()))
+    contract_rows = (((0,), (0,)), ((), ()))
+    minus_ones = jnp.full((ROWS, HEAD), -1.0, BF16)
+    scale_2 = softmax_scale * math.log2(math.e)
+
+    def heads(tensor, group):
+        return jnp.concatenate(
+            [
+                tensor[:, (group * WIDTH + h) * HEAD : (group * WIDTH + h + 1) * HEAD]
+                for h in range(WIDTH)
+            ],
+            axis=0,
+        )
+
+    def scores_of(keys, group, bias):
+        product = lax.dot_general(
+            keys, heads(q, group), contract_features, preferred_element_type=F32
+        )
+        return product * scale_2 + bias
+
+    def centred_of(values, group):
+        return lax.dot_general(
+            jnp.concatenate([values, minus_ones], axis=1),
+            with_products[group],
+            contract_features,
+            preferred_element_type=F32,
+        )
+
+    for group in range(GROUPS):
+        columns = slice(group * HEAD, (group + 1) * HEAD)
+        grads = heads(do, group)
+        products = (grads.astype(F32) * heads(o, group).astype(F32)).astype(BF16)
+        with_products[group] = jnp.concatenate([grads, products], axis=1)
+        scores[group] = scores_of(k[:, columns], group, own_bias)
+        centred[group] = centred_of(v[:, columns], group)
+
     @pl.when(first)
     def _():
         wait_bytes(arrived, route_sem)
@@ -231,45 +284,6 @@
             before.at[group_here, kind_here, rows_of(tile_here)],
             kv_recv.at[group_here],
         ).start()
-
-    for load in loads[2:]:
-        load.wait()
-
-    contract_features = (((1,), (1,)), ((), ()))
-    contract_rows = (((0,), (0,)), ((), ()))
-    minus_ones = jnp.full((ROWS, HEAD), -1.0, BF16)
-    scale_2 = softmax_scale * math.log2(math.e)
-
-    def heads(tensor, group):
-        return jnp.concatenate(
-            [
-                tensor[:, (group * WIDTH + h) * HEAD : (group * WIDTH + h + 1) * HEAD]
-                for h in range(WIDTH)
-            ],
-            axis=0,
-        )
-
-    def scores_of(keys, group, bias):
-        product = lax.dot_general(
-            keys, heads(q, group), contract_features, preferred_element_type=F32
-        )
-        return product * scale_2 + bias
-
-    def centred_of(values, group):
-        return lax.dot_general(
-            jnp.concatenate([values, minus_ones], axis=1),
-            with_products[group],
-            contract_features,
-            preferred_element_type=F32,
-        )
-
-    for group in range(GROUPS):
-        columns = slice(group * HEAD, (group + 1) * HEAD)
-        grads = heads(do, group)
-        products = (grads.astype(F32) * heads(o, group).astype(F32)).astype(BF16)
-        with_products[group] = jnp.concatenate([grads, products], axis=1)
-        scores[group] = scores_of(k[:, columns], group, own_bias)
-        centred[group] = centred_of(v[:, columns], group)
 
     for group in range(GROUPS):
         wait_bytes(before.at[group], kv_recv.at[group])
@@ -359,7 +373,7 @@
                 device_id_type=MESH,
             ).start()
 
-        for_others(me, pass_on)
+        for_others_mixed(me, pass_on)
         routed_back[me] = arrived_back[number_in(table_smem, 1, me)]
         pltpu.make_async_copy(
             routed_back.at[me],

time: 39.6 us -> 39.4 us (level)
  no operation moved by 1% of the time
where the time goes in v4:
time: 39.4 us; the launch traced here: 39.2 us
  Pallas kernels  38.6 us (98%)
  between operations  0.64 us (2%)
    pallas_call x1, Pallas kernels, per_device(): pl.pallas_call(kernel, out_shape=[pltpu.VMEM(wide, BF16), pltpu.VMEM(narr...  37.7 us
    pallas_call x1, Pallas kernels, per_device(): pl.pallas_call(store, out_shape=[jax.ShapeDtypeStruct(grad.shape, BF16) f...  0.9 us

profile of v4, /device:TPU:449, one launch (start us, length us, event | category | flops | bytes accessed | tf_op | source)
XLA Modules:
  0.0 39.2 jit_solution(1704327638252469553)
XLA Ops:
  0.6 37.7 %shard_map.94 = (bf16[128,2048]{1,0:T(8,128)(2,1)S(1)}, bf16[128,512]{1,0:T(8,128)(2,1)S(1)}, bf16[128,512]{1,0:T(8,128)(2,1)S(1)}) custom-call(s32[64]{0:T(128)} %stretch_order.1, s32[512,128]{1,0:T(8,128)} %bitcast.1, bf16[128,2048]{1,0:T(8,128)(2,1)} %query.1, bf16[128,512]{1,0:T(8,128)(2,1)} %key.1, bf16[128,512]{1,0:T(8,128)(2,1)} %value.1, ...), custom_call_target="tpu_custom_call" | custom-call | flops 671000000 | bytes 2700000 | tf_op jit(solution)/shard_map/pallas_call | solution.py:429
  38.3 0.9 %shard_map.95 = (bf16[128,2048]{1,0:T(8,128)(2,1)}, bf16[128,512]{1,0:T(8,128)(2,1)}, bf16[128,512]{1,0:T(8,128)(2,1)}) custom-call(bf16[128,2048]{1,0:T(8,128)(2,1)S(1)} %get-tuple-element.6.dq, bf16[128,512]{1,0:T(8,128)(2,1)S(1)} %get-tuple-element.7.dk, bf16[128,512]{1,0:T(8,128)(2,1)S(1)} %get-tuple-element.8.dv), custom_call_target="tpu_custom_call" | custom-call | tf_op jit(solution)/shard_map/pallas_call | solution.py:493

commit v5 on v4

--- a/solution.py
+++ b/solution.py
@@ -16,7 +16,7 @@
 STRETCHES = 64
 SEQUENCE = STRETCHES * RUN * ROWS
 TILE = 16
-Y_STEPS = (4, 1, 3, 7, 5, 2, 6, 0)
+Y_STEPS = (4, 3, 5, 2, 6, 1, 7, 0)
 NEGATIVE = -1e30
 MESH = pl.DeviceIdType.MESH
 F32 = jnp.float32

time: 39.4 us -> 39.2 us (level)
  no operation moved by 1% of the time
where the time goes in v5:
time: 39.2 us; the launch traced here: 39.1 us
  Pallas kernels  38.4 us (98%)
  between operations  0.64 us (2%)
    pallas_call x1, Pallas kernels, per_device(): pl.pallas_call(kernel, out_shape=[pltpu.VMEM(wide, BF16), pltpu.VMEM(narr...  37.5 us
    pallas_call x1, Pallas kernels, per_device(): pl.pallas_call(store, out_shape=[jax.ShapeDtypeStruct(grad.shape, BF16) f...  0.9 us

profile of v5, /device:TPU:449, one launch (start us, length us, event | category | flops | bytes accessed | tf_op | source)
XLA Modules:
  0.0 39.1 jit_solution(11137514604319478001)
XLA Ops:
  0.6 37.5 %shard_map.94 = (bf16[128,2048]{1,0:T(8,128)(2,1)S(1)}, bf16[128,512]{1,0:T(8,128)(2,1)S(1)}, bf16[128,512]{1,0:T(8,128)(2,1)S(1)}) custom-call(s32[64]{0:T(128)} %stretch_order.1, s32[512,128]{1,0:T(8,128)} %bitcast.1, bf16[128,2048]{1,0:T(8,128)(2,1)} %query.1, bf16[128,512]{1,0:T(8,128)(2,1)} %key.1, bf16[128,512]{1,0:T(8,128)(2,1)} %value.1, ...), custom_call_target="tpu_custom_call" | custom-call | flops 671000000 | bytes 2700000 | tf_op jit(solution)/shard_map/pallas_call | solution.py:429
  38.2 0.9 %shard_map.95 = (bf16[128,2048]{1,0:T(8,128)(2,1)}, bf16[128,512]{1,0:T(8,128)(2,1)}, bf16[128,512]{1,0:T(8,128)(2,1)}) custom-call(bf16[128,2048]{1,0:T(8,128)(2,1)S(1)} %get-tuple-element.6.dq, bf16[128,512]{1,0:T(8,128)(2,1)S(1)} %get-tuple-element.7.dk, bf16[128,512]{1,0:T(8,128)(2,1)S(1)} %get-tuple-element.8.dv), custom_call_target="tpu_custom_call" | custom-call | tf_op jit(solution)/shard_map/pallas_call | solution.py:493
